TPU v7x, 32 devices: a whole 2x2x4 slice. The times are simulated.
32 devices in a mesh: tok: 4 (over x, core), wa: 8 (over z, y).
Axes of the slice: x: 2, y: 2, z: 4, core: 2. Of those that a mesh axis runs over, the one named last changes fastest.
Arguments:
- tokens: bfloat16 [2048, 8192], P('tok', 'wa'), may hold values from -6 to 6
- gate_weight: bfloat16 [224, 8, 128, 128], P('wa', 'tok'), may hold values from -0.1875 to 0.1875
- up_weight: bfloat16 [224, 8, 128, 128], P('wa', 'tok'), may hold values from -0.1875 to 0.1875
- down_weight: bfloat16 [64, 24, 128, 128], P('wa', 'tok'), may hold values from -0.109375 to 0.109375
- gate_list: int32 [224, 8], P('wa'), may hold values from -1 to 63, as said below
- up_list: int32 [224, 8], P('wa'), may hold values from -1 to 63, as said below
- down_list: int32 [64, 24], replicated, may hold values from -1 to 223, as said below
Outputs:
- mixed_out: bfloat16 [2048, 8192], P('tok', 'wa')
Inputs may be any that keep to these rules, and one draw needn't show every extreme that they name: `gate_list`: row j lists distinct feature blocks in ascending order followed by -1; each row has 4 to 8 entries and some row exactly 8. `up_list`: row j lists distinct feature blocks in ascending order followed by -1; each row has 4 to 8 entries and some row exactly 8. `down_list`: row c lists distinct hidden blocks in ascending order followed by -1; each row has 18 to 24 entries and some row exactly 24. Each aligned group of 8 rows names at most 4 distinct blocks of any aligned range of 28 hidden blocks, and every group names exactly 4 of some range.
All inputs are finite; a program needn't handle non-finite values.
Results may differ from a plain program's by a relative error of at most 0.0049.
Values may be sent and summed in bfloat16 or wider, within the bound.
A program may use at most 192 MiB of HBM per device.

v0:
```python
import jax
import jax.numpy as jnp
from jax import lax
from jax.sharding import PartitionSpec as P


def listed_product(source_blocks, weights, block_lists):
    present = (block_lists >= 0).astype(jnp.bfloat16)
    picked = jnp.take(source_blocks, jnp.maximum(block_lists, 0), axis=1)
    picked = picked * present[None, :, :, None]
    return jnp.einsum("rckm,ckmn->rcn", picked, weights, preferred_element_type=jnp.float32)


def on_device(tokens, gate_weight, up_weight, down_weight, gate_list, up_list, down_list):
    gate_full, up_full, down_full = (
        lax.all_gather(gate_weight, "tok", axis=1, tiled=True),
        lax.all_gather(up_weight, "tok", axis=1, tiled=True),
        lax.all_gather(down_weight, "tok", axis=1, tiled=True),
    )
    features = lax.all_gather(tokens, "wa", axis=1, tiled=True)
    row_count = features.shape[0]
    block_size = gate_full.shape[2]
    feature_blocks = features.reshape(row_count, -1, block_size)
    gate_sum = listed_product(feature_blocks, gate_full, gate_list)
    up_sum = listed_product(feature_blocks, up_full, up_list)
    hidden = (jax.nn.silu(gate_sum) * up_sum).astype(jnp.bfloat16)
    wa_size = lax.axis_size("wa")
    my_index = lax.axis_index("wa")
    out_blocks = down_full.shape[0]
    slot_count = down_full.shape[1]
    hid_blocks = hidden.shape[1]
    my_lists = lax.dynamic_slice_in_dim(down_list, my_index * out_blocks, out_blocks, 0)
    capacity = max(2, (slot_count + wa_size - 1) // wa_size + 1)
    group_lists = down_list.reshape(wa_size, -1)
    own_ids = my_index * hid_blocks + jnp.arange(hid_blocks, dtype=jnp.int32)
    wanted = jnp.any(group_lists[:, :, None] == own_ids[None, None, :], axis=1)
    places = jnp.cumsum(wanted.astype(jnp.int32), axis=1) - 1
    slot_ids = jnp.arange(capacity, dtype=jnp.int32)
    select = (wanted[:, None, :] & (places[:, None, :] == slot_ids[None, :, None])).astype(
        jnp.bfloat16
    )
    outgoing = jnp.einsum(
        "scb,rbm->scrm", select, hidden, preferred_element_type=jnp.float32
    ).astype(jnp.bfloat16)
    incoming = lax.all_to_all(outgoing, "wa", split_axis=0, concat_axis=0, tiled=True)
    all_ids = jnp.arange(wa_size * hid_blocks, dtype=jnp.int32)
    mine_wanted = jnp.any(my_lists.reshape(-1)[:, None] == all_ids[None, :], axis=0)
    mine_wanted = mine_wanted.reshape(wa_size, hid_blocks)
    my_places = (jnp.cumsum(mine_wanted.astype(jnp.int32), axis=1) - 1).reshape(-1)
    safe_ids = jnp.maximum(my_lists, 0)
    owners = safe_ids // hid_blocks
    slot_index = jnp.maximum(owners * capacity + jnp.take(my_places, safe_ids), 0)
    present = (my_lists >= 0).astype(jnp.bfloat16)
    received = incoming.reshape(wa_size * capacity, row_count, block_size)
    picked = jnp.take(received, slot_index, axis=0)
    picked = picked * present[:, :, None, None]
    mixed_out = jnp.einsum("ckrm,ckmn->rcn", picked, down_full, preferred_element_type=jnp.float32)
    return mixed_out.reshape(row_count, out_blocks * block_size).astype(jnp.bfloat16)


def solution(mesh):
    placed = (
        P("tok", "wa"),
        P("wa", "tok", None, None),
        P("wa", "tok", None, None),
        P("wa", "tok", None, None),
        P("wa", None),
        P("wa", None),
        P(),
    )
    return jax.shard_map(
        on_device, mesh=mesh, in_specs=placed, out_specs=P("tok", "wa"), check_vma=False
    )
```

profile of v0, /device:TPU:0, one launch (start us, length us, event | category | flops | bytes accessed | tf_op | source)
XLA Modules:
  0.0 402.1 jit_solution(11962701419793197618)
XLA Ops:
  6.5 0.0 all-gather.5.cloned.1.call-start
  6.5 2.3 copy.82
  8.9 0.0 all-gather.5.cloned.1.call-update
  8.9 0.0 all-gather.7.cloned.1.call-start
  8.9 0.7 all-gather.7.cloned.1.call-update
  9.6 0.0 all-gather.9.cloned.1.call-start
  9.7 0.7 all-gather.9.cloned.1.call-update
  10.4 0.0 all-gather.11.cloned.1.call-start
  10.4 2.6 copy.92
  13.0 0.0 all-gather.11.cloned.1.call-update
  13.1 0.0 copy-done.2
  13.1 0.1 copy.77
  13.2 0.1 copy.83
  13.3 0.1 reshape.92
  13.4 0.1 copy.85
  13.5 0.1 copy.81
  13.6 0.1 copy.87
  13.7 0.1 reshape.96
  13.8 0.1 copy.89
  13.9 0.1 copy.86
  14.0 0.1 eq.47
  14.1 0.6 compare_reduce_fusion
  14.7 0.1 copy.79
  14.8 0.2 reduce_window_sum.18
  15.0 122.1 %all-gather.5.cloned.1.call-done = bf16[512,8192]{0,1:T(8,128)(2,1)} async-done(((bf16[512,1024]{0,1:T(8,128)(2,1)}), bf16[512,8192]{0,1:T(8,128)(2,1)}) %all-gather.5.cloned.1.call-update) | async-done | bytes 8388624 | tf_op jit(solution)/shard_map/all_gather | solution.py:20
  137.2 12.1 %copy.84 = bf16[512,64,128]{2,0,1:T(8,128)(2,1)} copy(bf16[512,64,128]{0,2,1:T(8,128)(2,1)} %bitcast.58) | data formatting | bytes 16777216 | tf_op jit(solution)/shard_map/reshape | solution.py:23
  149.2 15.7 %gather_fusion.2 = bf16[224,512,128]{2,1,0:T(8,128)(2,1)} fusion(bf16[512,64,128]{2,0,1:T(8,128)(2,1)} %copy.84, s32[1024]{0:T(1024)S(1)} %pad_clamp_fusion.2), kind=kCustom, calls=%fused_computation.clone | custom fusion | bytes 58721152 | tf_op jit(solution)/shard_map/jit(_take)/gather | solution.py:9
  164.9 15.7 %gather_fusion.3 = bf16[224,512,128]{2,1,0:T(8,128)(2,1)} fusion(bf16[512,64,128]{2,0,1:T(8,128)(2,1)} %copy.84, s32[1024]{0:T(1024)S(1)} %pad_clamp_fusion.1), kind=kCustom, calls=%fused_computation.1.clone | custom fusion | bytes 58721152 | tf_op jit(solution)/shard_map/jit(_take)/gather | solution.py:9
  180.6 8.7 %all-gather.7.cloned.1.call-done = bf16[28,8,128,128]{3,2,1,0:T(8,128)(2,1)} async-done(((bf16[28,2,128,128]{3,2,1,0:T(8,128)(2,1)}), bf16[28,8,128,128]{3,2,1,0:T(8,128)(2,1)}) %all-gather.7.cloned.1.call-update) | async-done | bytes 7340048 | tf_op jit(solution)/shard_map/all_gather | solution.py:16
  189.3 20.4 %fusion.1 = f32[28,512,128,1]{2,1,3,0:T(8,128)} fusion(bf16[28,8,128,128]{3,2,1,0:T(8,128)(2,1)} %all-gather.7.cloned.1.call-done, bf16[28,8,512,128]{3,2,1,0:T(8,128)(2,1)} %bitcast.56, pred[28,8]{1,0:T(8,128)(4,1)S(1)} %copy.81, bf16[28,8]{1,0:T(8,128)(2,1)S(1)} %copy.85), kind=kOutput, calls=%fused_computation.7 | convolution fusion | flops 3787456512 | bytes 44040864 | tf_op jit(solution)/shard_map/rckm,ckmn->rcn/dot_general | solution.py:11
  209.7 33.5 %all-gather.9.cloned.1.call-done = bf16[28,8,128,128]{3,2,1,0:T(8,128)(2,1)} async-done(((bf16[28,2,128,128]{3,2,1,0:T(8,128)(2,1)}), bf16[28,8,128,128]{3,2,1,0:T(8,128)(2,1)}) %all-gather.9.cloned.1.call-update) | async-done | bytes 7340048 | tf_op jit(solution)/shard_map/all_gather | solution.py:17
  243.2 19.0 %fusion.16 = bf16[512,28,128]{2,0,1:T(8,128)(2,1)S(1)} fusion(f32[28,512,128,1]{2,1,3,0:T(8,128)} %fusion.1, bf16[28,8,128,128]{3,2,1,0:T(8,128)(2,1)} %all-gather.9.cloned.1.call-done, bf16[28,8,512,128]{3,2,1,0:T(8,128)(2,1)} %bitcast.55, pred[28,8]{1,0:T(8,128)(4,1)S(1)} %copy.86, bf16[28,8]{1,0:T(8,128)(2,1)S(1)} %copy.89), kind=kOutput, calls=%fused_computation.23 | convolution fusion | flops 3798466560 | bytes 47710880 | tf_op jit(solution)/shard_map/rckm,ckmn->rcn/dot_general | solution.py:11
  262.2 2.3 fusion.23
  264.5 2.9 copy.91
  267.5 5.5 %all-to-all-start = ((bf16[8,4,512,128]{3,2,1,0:T(8,128)(2,1)}), bf16[8,4,512,128]{3,2,1,0:T(8,128)(2,1)}, u32[]{:S(2)}, u32[]{:S(2)}) async-start(bf16[8,4,512,128]{3,2,1,0:T(8,128)(2,1)} %copy.91), calls=%async_computation | async-start | bytes 8388608 | tf_op jit(solution)/shard_map/all_to_all | solution.py:45
  272.9 0.1 eq.43
  273.0 0.1 fusion.28
  273.1 0.1 reshape.51
  273.2 0.2 reduce_window_sum.17
  273.4 0.1 sub.16
  273.5 0.1 reshape.70
  273.6 1.6 gather_fusion
  275.2 0.1 reshape.69
  275.3 0.1 reshape.78
  275.4 91.2 %all-to-all-done = bf16[8,4,512,128]{3,2,1,0:T(8,128)(2,1)} async-done(((bf16[8,4,512,128]{3,2,1,0:T(8,128)(2,1)}), bf16[8,4,512,128]{3,2,1,0:T(8,128)(2,1)}, u32[]{:S(2)}, u32[]{:S(2)}) %all-to-all-start) | async-done | bytes 4194336 | tf_op jit(solution)/shard_map/all_to_all | solution.py:45
  366.6 13.3 %gather_fusion.1 = bf16[192,512,128]{2,1,0:T(8,128)(2,1)} fusion(bf16[32,512,128]{2,1,0:T(8,128)(2,1)} %bitcast.15, s32[1024]{0:T(1024)S(1)} %pad_clamp_fusion), kind=kCustom, calls=%fused_computation.3 | custom fusion | bytes 50332416 | tf_op jit(solution)/shard_map/jit(_take)/gather | solution.py:55
  380.0 14.3 %bitcast_convert_fusion = bf16[8,512,128]{1,2,0:T(8,128)(2,1)S(1)} fusion(bf16[8,24,128,128]{2,3,1,0:T(8,128)(2,1)} %all-gather.11.cloned.1.call-done, bf16[8,24,512,128]{3,2,1,0:T(8,128)(2,1)} %bitcast.57, pred[8,24]{1,0:T(8,128)(4,1)S(1)} %get-tuple-element.8, bf16[8,24]{1,0:T(8,128)(2,1)S(1)} %get-tuple-element.6), kind=kOutput, calls=%fused_computation.33 | convolution fusion | flops 3246915584 | bytes 32506432 | tf_op jit(solution)/shard_map/ckrm,ckmn->rcn/dot_general | solution.py:57
  394.2 1.3 copy.93
  (22 shorter events, 0.1 us)
Async XLA Ops:
  6.5 6.5 %copy-start = (s32[28,8]{0,1:T(8,128)S(1)}, s32[28,8]{0,1:T(8,128)}, u32[]{:S(2)}) copy-start(s32[28,8]{0,1:T(8,128)} %param.13) | copy-start | bytes 2692
  6.5 6.6 %copy-start.1 = (s32[28,8]{0,1:T(8,128)S(1)}, s32[28,8]{0,1:T(8,128)}, u32[]{:S(2)}) copy-start(s32[28,8]{0,1:T(8,128)} %param.14) | copy-start | bytes 2692
  6.5 6.6 %copy-start.2 = (s32[64,24]{0,1:T(8,128)S(1)}, s32[64,24]{0,1:T(8,128)}, u32[]{:S(2)}) copy-start(s32[64,24]{0,1:T(8,128)} %param.15) | copy-start | bytes 18436
  6.5 130.6 %all-gather.5.cloned.1.call-start = ((), (), s32[]{:S(2)}) async-start(), calls=%async_computation.1 | async-start | bytes 9437184 | tf_op jit(solution)/shard_map/all_gather | solution.py:20
  8.9 180.4 %all-gather.7.cloned.1.call-start = ((), (), s32[]{:S(2)}) async-start(), calls=%async_computation.2 | async-start | bytes 9175040 | tf_op jit(solution)/shard_map/all_gather | solution.py:16
  9.6 233.6 %all-gather.9.cloned.1.call-start = ((), (), s32[]{:S(2)}) async-start(), calls=%async_computation.3 | async-start | bytes 9175040 | tf_op jit(solution)/shard_map/all_gather | solution.py:17
  10.4 369.6 %all-gather.11.cloned.1.call-start = ((), (), s32[]{:S(2)}) async-start(), calls=%async_computation.4 | async-start | bytes 7864320 | tf_op jit(solution)/shard_map/all_gather | solution.py:18
  267.5 99.2 %all-to-all-start = ((bf16[8,4,512,128]{3,2,1,0:T(8,128)(2,1)}), bf16[8,4,512,128]{3,2,1,0:T(8,128)(2,1)}, u32[]{:S(2)}, u32[]{:S(2)}) async-start(bf16[8,4,512,128]{3,2,1,0:T(8,128)(2,1)} %copy.91), calls=%async_computation | async-start | bytes 8388608 | tf_op jit(solution)/shard_map/all_to_all | solution.py:45
Sparse Core Ops, SparseCore 0:
  9.5 127.6 all-gather.4
  138.7 50.4 all-gather.6
  190.8 52.3 all-gather.8
  244.6 46.3 all-gather.10
where the time goes:
time: 403 us; the launch traced here: 402 us
  waiting for transfers between devices  257 us (64%)
  local copies, waits for them, and re-layouts  69 us (17%)
  matrix products  56 us (14%)
  between operations  13.3 us (3%)
  starting transfers between devices  5.6 us (1%)
    all_gather x1, waiting for transfers between devices, on_device(): features = lax.all_gather(tokens, 'wa', axis=1, tiled=True)  122 us
    all_to_all x1, waiting for transfers between devices, on_device(): lax.all_to_all(outgoing, 'wa', split_axis=0, concat_axis=0, tiled=True)  91.2 us
    dot_general x2, matrix products, listed_product(): jnp.einsum('rckm,ckmn->rcn', picked, weights, preferred_element_type=jnp....  39.4 us
    all_gather x1, waiting for transfers between devices, on_device(): lax.all_gather(up_weight, 'tok', axis=1, tiled=True)  33.5 us
    gather x2, local copies, waits for them, and re-layouts, listed_product(): picked = jnp.take(source_blocks, jnp.maximum(block_lists, 0), axis=1)  31.4 us
    dot_general x1, matrix products, on_device(): jnp.einsum('ckrm,ckmn->rcn', picked, down_full, preferred_element_type=jn...  14.3 us
    gather x1, local copies, waits for them, and re-layouts, on_device(): picked = jnp.take(received, slot_index, axis=0)  13.3 us
    reshape x1, local copies, waits for them, and re-layouts, on_device(): feature_blocks = features.reshape(row_count, -1, block_size)  12.1 us
  transfers between devices with their start and end apart: 5, of which 4 were waited for; matrix products, arithmetic and copies ran while one was open for 27% of the time, Pallas kernels for 0%

commit v1 on v0

v1 whole, which is shorter than its diff:
```python
import functools

import jax
import jax.numpy as jnp
from jax import lax
from jax.experimental import pallas as pl
from jax.experimental.pallas import tpu as pltpu
from jax.sharding import PartitionSpec as P

MESH = pl.DeviceIdType.MESH


def exchange_kernel(
    sizes, ids_ref, rows_ref, tok_ref, gate_ref, up_ref, down_ref,
    feat_ref, got_ref, down_out, rows_out,
    sel, zero, zr_s, zr_r, zl_s, zl_r, y_s, y_r, wx_s, wx_r, li_s, li_r, xs_s, xs_r, sib_s, sib_r, loc,
):
    nt, nw, cap = sizes
    xs, ys = nt // 2, nt // 2
    zs = nw // ys
    t, w = lax.axis_index("tok"), lax.axis_index("wa")
    x, c = lax.div(t, 2), lax.rem(t, 2)
    z, y = lax.div(w, ys), lax.rem(w, ys)
    fb = tok_ref.shape[0]

    barrier = pltpu.get_barrier_semaphore()
    for r in range(1, nw):
        pl.semaphore_signal(barrier, inc=1, device_id=(t, lax.rem(w + r, nw)), device_id_type=MESH)
    for r in range(1, nt):
        pl.semaphore_signal(barrier, inc=1, device_id=(lax.rem(t + r, nt), w), device_id_type=MESH)
    pl.semaphore_wait(barrier, nw + nt - 2)

    def remote(src, dst, ssem, rsem, dev):
        return pltpu.make_async_remote_copy(
            src_ref=src, dst_ref=dst, send_sem=ssem, recv_sem=rsem, device_id=dev, device_id_type=MESH
        )

    def feat(src):
        return feat_ref.at[pl.ds(src * fb, fb)]

    def right(k, src):
        return remote(src, feat(w - (k - 1) * ys), zr_s.at[k - 1], zr_r.at[k - 1], (t, w + ys))

    def left(k, src):
        return remote(src, feat(w + (k - 1) * ys), zl_s.at[k - 1], zl_r.at[k - 1], (t, w - ys))

    def across(zz, dy, src):
        return remote(
            src, feat(zz * ys + y), y_s.at[zz, dy - 1], y_r.at[zz, dy - 1], (t, z * ys + lax.rem(y + dy, ys))
        )

    def send_right(k, src):
        pl.when((z + 1 < zs) & (z - (k - 1) >= 0))(lambda: right(k, src).start())

    def send_left(k, src):
        pl.when((z >= 1) & (z + (k - 1) < zs))(lambda: left(k, src).start())

    send_right(1, tok_ref)
    send_left(1, tok_ref)
    for dy in range(1, ys):
        across(z, dy, tok_ref).start()

    def sibling(j, e, src, dst):
        return remote(src, dst, sib_s.at[j, e], sib_r.at[j, e], (x * 2 + (1 - c), w))

    def along_x(j, dx, src, dst):
        return remote(src, dst, xs_s.at[j, dx - 1], xs_r.at[j, dx - 1], (lax.rem(x + dx, xs) * 2 + c, w))

    def source(j):
        return lax.rem(w + nw - j, nw)

    def slot(j, tt):
        return down_out.at[tt] if j == nw else got_ref.at[tt, source(j)]

    def from_x(dx):
        return lax.rem(x + xs - dx, xs) * 2 + c

    def spread(j, src):
        for dx in range(1, xs):
            along_x(j, dx, src, slot(j, t)).start()
        sibling(j, 0, src, slot(j, t)).start()

    spread(nw, down_ref)

    zero[...] = jnp.zeros_like(zero)
    own_copies = [
        pltpu.make_async_copy(zero, feat_ref.at[nw * fb], loc.at[0]),
        pltpu.make_async_copy(tok_ref, feat(w), loc.at[1]),
        pltpu.make_async_copy(down_ref, down_out.at[t], loc.at[2]),
        pltpu.make_async_copy(sel.at[w], got_ref.at[t, w], loc.at[3]),
        pltpu.make_async_copy(rows_ref.at[w], rows_out.at[w], loc.at[4]),
    ]
    for copy in own_copies[:3]:
        copy.start()

    def pick(d):
        for s in range(cap):
            chosen = ids_ref[d * cap + s]
            sel[d, s, 0] = gate_ref[chosen]
            sel[d, s, 1] = up_ref[chosen]

    pick(w)
    own_copies[3].start()
    own_copies[4].start()
    spread(0, sel.at[w])

    def to_dest(r):
        return remote(
            sel.at[lax.rem(w + r, nw)], got_ref.at[t, w], wx_s.at[r - 1], wx_r.at[r - 1], (t, lax.rem(w + r, nw))
        )

    def rows_to_dest(r):
        return remote(
            rows_ref.at[lax.rem(w + r, nw)], rows_out.at[w], li_s.at[r - 1], li_r.at[r - 1], (t, lax.rem(w + r, nw))
        )

    for r in range(1, nw):
        pick(lax.rem(w + r, nw))
        to_dest(r).start()
        rows_to_dest(r).start()

    def forward_tokens(k):
        @pl.when(z - k >= 0)
        def _():
            block = feat(w - k * ys)
            remote(block, block, zr_s.at[k - 1], zr_r.at[k - 1], (t, w)).wait_recv()
            if k < zs - 1:
                send_right(k + 1, block)
            for dy in range(1, ys):
                across(z - k, dy, block).start()

        @pl.when(z + k < zs)
        def _():
            block = feat(w + k * ys)
            remote(block, block, zl_s.at[k - 1], zl_r.at[k - 1], (t, w)).wait_recv()
            if k < zs - 1:
                send_left(k + 1, block)
            for dy in range(1, ys):
                across(z + k, dy, block).start()

    def forward_weights(j):
        to_me = got_ref.at[t, source(j)]
        remote(to_me, to_me, wx_s.at[j - 1], wx_r.at[j - 1], (t, w)).wait_recv()
        spread(j, to_me)

    def forward_sibling(j):
        for dx in range(1, xs):
            there = slot(j, from_x(dx))
            along_x(j, dx, there, there).wait_recv()
            sibling(j, dx, there, there).start()

    forward_sibling(nw)
    per = -(-(nw - 1) // (zs - 1))
    for k in range(1, zs):
        forward_tokens(k)
        for j in range((k - 1) * per + 1, min(k * per, nw - 1) + 1):
            forward_weights(j)
            forward_sibling(j - 1)
    forward_sibling(nw - 1)

    for zz in range(zs):
        for dy in range(1, ys):
            block = feat(zz * ys + lax.rem(y + ys - dy, ys))
            across(zz, dy, block).wait_recv()
    for r in range(1, nw):
        row = rows_out.at[source(r)]
        remote(row, row, li_s.at[r - 1], li_r.at[r - 1], (t, w)).wait_recv()
    for j in [*range(nw), nw]:
        other = x * 2 + (1 - c)
        sibling(j, 0, slot(j, other), slot(j, other)).wait_recv()
        for dx in range(1, xs):
            there = slot(j, lax.rem(x + xs - dx, xs) * 2 + (1 - c))
            sibling(j, dx, there, there).wait_recv()
    for copy in own_copies:
        copy.wait()
    for k in range(1, zs):
        pl.when((z + 1 < zs) & (z - (k - 1) >= 0))(lambda: right(k, tok_ref).wait_send())
        pl.when((z >= 1) & (z + (k - 1) < zs))(lambda: left(k, tok_ref).wait_send())
    for zz in range(zs):
        for dy in range(1, ys):
            across(zz, dy, tok_ref).wait_send()
    for r in range(1, nw):
        to_dest(r).wait_send()
        rows_to_dest(r).wait_send()
    for j in [*range(nw), nw]:
        for dx in range(1, xs):
            along_x(j, dx, slot(j, t), slot(j, t)).wait_send()
        for e in range(xs):
            sibling(j, e, slot(j, t), slot(j, t)).wait_send()


def exchange(sizes, ids, rows, tokens, gate, up, down):
    nt, nw, cap = sizes
    fb, row_count, blk = tokens.shape
    slots = gate.shape[1]
    xs = ys = nt // 2
    zs = nw // ys
    sem = pltpu.SemaphoreType.DMA
    dtype = tokens.dtype
    any_spec = pl.BlockSpec(memory_space=pl.ANY)
    vmem_spec = pl.BlockSpec(memory_space=pltpu.VMEM)
    return pl.pallas_call(
        functools.partial(exchange_kernel, sizes),
        out_shape=(
            jax.ShapeDtypeStruct((nw * fb + 1, row_count, blk), dtype),
            jax.ShapeDtypeStruct((nt, nw, cap, 2, slots, blk, blk), dtype),
            jax.ShapeDtypeStruct((nt, *down.shape), dtype),
            jax.ShapeDtypeStruct(rows.shape, rows.dtype),
        ),
        in_specs=[pl.BlockSpec(memory_space=pltpu.SMEM), any_spec, any_spec, vmem_spec, vmem_spec, any_spec],
        out_specs=(any_spec,) * 4,
        scratch_shapes=[
            pltpu.VMEM((nw, cap, 2, slots, blk, blk), dtype),
            pltpu.VMEM((row_count, blk), dtype),
            sem((zs - 1,)), sem((zs - 1,)), sem((zs - 1,)), sem((zs - 1,)),
            sem((zs, ys - 1)), sem((zs, ys - 1)),
            sem((nw - 1,)), sem((nw - 1,)), sem((nw - 1,)), sem((nw - 1,)),
            sem((nw + 1, xs - 1)), sem((nw + 1, xs - 1)), sem((nw + 1, xs)), sem((nw + 1, xs)),
            sem((5,)),
        ],
        compiler_params=pltpu.CompilerParams(
            collective_id=0, has_side_effects=True, vmem_limit_bytes=24 << 20
        ),
    )(ids, rows, tokens, gate, up, down)


def layer_kernel(sizes, rows_ref, places_ref, feat_ref, got_ref, down_ref, out_ref, hidden):
    nt, nw, cap, kg, kd, none = sizes
    step = pl.program_id(0)
    blk = feat_ref.shape[2]

    def column(s, which):
        base = ((step * cap + s) * 2 + which) * kg
        lhs = jnp.concatenate([feat_ref[rows_ref[base + k]] for k in range(kg)], axis=1)
        rhs = jnp.concatenate([got_ref[tt, 0, s, which].reshape(-1, blk) for tt in range(nt)], axis=0)
        return jnp.dot(lhs, rhs, preferred_element_type=jnp.float32)

    @pl.when(step == 0)
    def _():
        hidden[nw * cap] = jnp.zeros(hidden.shape[1:], hidden.dtype)

    for s in range(cap):
        gate = column(s, 0)
        up = column(s, 1)
        hidden[step * cap + s] = (gate / (1.0 + jnp.exp(-gate)) * up).astype(hidden.dtype)

    @pl.when(step == nw - 1)
    def _():
        for b in range(out_ref.shape[1] // blk):
            lhs = jnp.concatenate([hidden[places_ref[b * kd + k]] for k in range(kd)], axis=1)
            rhs = jnp.concatenate([down_ref[tt, b].reshape(-1, blk) for tt in range(nt)], axis=0)
            out_ref[:, b * blk : (b + 1) * blk] = jnp.dot(
                lhs, rhs, preferred_element_type=jnp.float32
            ).astype(out_ref.dtype)


def layer(sizes, rows, places, feat, got, down):
    nt, nw, cap, kg, kd, none = sizes
    row_count, blk = feat.shape[1:]
    outs = down.shape[1]
    vmem_spec = pl.BlockSpec(memory_space=pltpu.VMEM)
    return pl.pallas_call(
        functools.partial(layer_kernel, sizes),
        out_shape=jax.ShapeDtypeStruct((row_count, outs * blk), feat.dtype),
        grid_spec=pltpu.PrefetchScalarGridSpec(
            num_scalar_prefetch=2,
            grid=(nw,),
            in_specs=[
                vmem_spec,
                pl.BlockSpec((nt, 1, *got.shape[2:]), lambda i, a, b: (0, i, 0, 0, 0, 0, 0)),
                vmem_spec,
            ],
            out_specs=pl.BlockSpec((row_count, outs * blk), lambda i, a, b: (0, 0)),
            scratch_shapes=[pltpu.VMEM((nw * cap + 1, row_count, blk), feat.dtype)],
        ),
        compiler_params=pltpu.CompilerParams(vmem_limit_bytes=48 << 20),
    )(rows, places, feat, got, down)


def running(flags):
    upto = jnp.arange(flags.shape[1])
    upto = upto[:, None] >= upto[None, :]
    return jnp.sum((flags[:, None, :] & upto[None]).astype(jnp.int32), axis=2)


def on_device(tokens, gate_weight, up_weight, down_weight, gate_list, up_list, down_list):
    nt, nw = lax.axis_size("tok"), lax.axis_size("wa")
    me = lax.axis_index("wa")
    hid_blocks, _, blk, _ = gate_weight.shape
    outs = down_weight.shape[0]
    kd, kg = down_list.shape[1], gate_list.shape[1]
    cap = max(2, (kd + nw - 1) // nw + 1)
    row_count = tokens.shape[0]
    fb = tokens.shape[1] // blk
    groups = down_list.reshape(nw, -1)

    own_ids = me * hid_blocks + jnp.arange(hid_blocks, dtype=jnp.int32)
    wanted = jnp.any(groups[:, :, None] == own_ids[None, None, :], axis=1)
    places = running(wanted) - 1
    chosen = wanted[:, None, :] & (places[:, None, :] == jnp.arange(cap, dtype=jnp.int32)[None, :, None])
    ids = jnp.sum(jnp.where(chosen, jnp.arange(hid_blocks, dtype=jnp.int32), 0), axis=2)
    both = jnp.concatenate([gate_list, up_list], axis=1)
    both = jnp.where(both < 0, nw * fb, both)
    picked = jnp.sum(jnp.where(chosen[..., None], both[None, None], 0), axis=2).reshape(nw, -1)
    width = -(-picked.shape[1] // 1024) * 1024
    rows = jnp.pad(picked, ((0, 0), (0, width - picked.shape[1]))).reshape(nw, -1, 128)

    mine = lax.dynamic_slice_in_dim(down_list, me * outs, outs, 0)
    all_ids = jnp.arange(nw * hid_blocks, dtype=jnp.int32)
    hit = mine.reshape(-1)[:, None] == all_ids[None, :]
    named = jnp.any(hit, axis=0).reshape(nw, hid_blocks)
    spot = running(named) - 1 + cap * jnp.arange(nw, dtype=jnp.int32)[:, None]
    spots = jnp.sum(jnp.where(hit, spot.reshape(1, -1), 0), axis=1)
    spots = jnp.where(mine.reshape(-1) >= 0, spots, nw * cap)

    blocks = jnp.transpose(tokens.reshape(row_count, fb, blk), (1, 0, 2))
    feat, got, down, got_rows = exchange(
        (nt, nw, cap), ids.reshape(-1), rows, blocks, gate_weight, up_weight, down_weight
    )
    lists = got_rows.reshape(nw, -1)[:, : cap * 2 * kg].reshape(-1)
    return layer((nt, nw, cap, kg, kd, nw * fb), lists, spots, feat, got, down)


def solution(mesh):
    placed = (
        P("tok", "wa"),
        P("wa", "tok", None, None),
        P("wa", "tok", None, None),
        P("wa", "tok", None, None),
        P("wa", None),
        P("wa", None),
        P(),
    )
    return jax.shard_map(
        on_device, mesh=mesh, in_specs=placed, out_specs=P("tok", "wa"), check_vma=False
    )
```

time: 403 us -> 244 us (0.61)
  waiting for transfers between devices: 257 us -> 0 us
  Pallas kernels: 0 us -> 224 us
  matrix products: 56 us -> 0 us
  local copies, waits for them, and re-layouts: 69 us -> 16.5 us
  between operations: 13.3 us -> 0.09 us
  starting transfers between devices: 5.6 us -> 0 us
    pallas_call x0 -> x2, Pallas kernels: none -> 224 us  [the longest x1 191 us: exchange(): pl.pallas_call(functools.partial(exchange_kernel, sizes), out_shape=(jax....]
    all_gather x4 -> x0, waiting for transfers between devices: 164 us -> none  [the longest x1 122 us: on_device(): features = lax.all_gather(tokens, 'wa', axis=1, tiled=True)]
    all_to_all x1 -> x0, waiting for transfers between devices: 91.2 us -> none  [on_device(): lax.all_to_all(outgoing, 'wa', split_axis=0, concat_axis=0, tiled=True)]
    dot_general x4 -> x0, matrix products: 56 us -> none  [the longest x2 39.4 us: listed_product(): jnp.einsum('rckm,ckmn->rcn', picked, weights, preferred_element_type=jnp....]
    gather x5 -> x0, local copies, waits for them, and re-layouts: 46.4 us -> none  [the longest x2 31.4 us: listed_product(): picked = jnp.take(source_blocks, jnp.maximum(block_lists, 0), axis=1)]
    reshape x1 -> x5, local copies, waits for them, and re-layouts: 12.1 us -> 0.98 us  [the longest x1 0.66 us: on_device(): blocks = jnp.transpose(tokens.reshape(row_count, fb, blk), (1, 0, 2))]
    unnamed x9 -> x16, local copies, waits for them, and re-layouts: 5.01 us -> 13.4 us
    all_to_all x1 -> x0, starting transfers between devices: 5.48 us -> none  [on_device(): lax.all_to_all(outgoing, 'wa', split_axis=0, concat_axis=0, tiled=True)]
  transfers between devices with their start and end apart: 5 -> 0, of which waited for: 4 -> 0; matrix products, arithmetic and copies ran while one was open for 27% -> 0% of each run, Pallas kernels for 0% -> 0%
where the time goes in v1:
time: 244 us
  Pallas kernels  224 us (92%)
  local copies, waits for them, and re-layouts  16.5 us (7%)
  other arithmetic  2.86 us (1%)
    pallas_call x1, Pallas kernels, exchange(): pl.pallas_call(functools.partial(exchange_kernel, sizes), out_shape=(jax....  191 us
    pallas_call x1, Pallas kernels, layer(): pl.pallas_call(functools.partial(layer_kernel, sizes), out_shape=jax.Shap...  33.1 us
    unnamed x16, local copies, waits for them, and re-layouts  13.4 us

profile of v1, /device:TPU:0, one launch (start us, length us, event | category | flops | bytes accessed | tf_op | source)
XLA Modules:
  0.0 243.7 jit_solution(10022456680953410505)
XLA Ops:
  0.0 0.7 constant_dynamic-update-slice_fusion.1
  0.7 0.7 constant_dynamic-update-slice_fusion
  1.4 0.8 constant_dynamic-slice_fusion
  2.2 0.1 copy.41
  2.2 0.1 reshape.103
  2.3 0.1 fusion
  2.5 0.1 and.46
  2.5 0.8 copy.33
  3.3 0.1 eq.45
  3.4 0.6 compare_reduce_fusion
  4.0 0.1 copy.34
  4.1 1.0 convert_reduce_fusion
  5.2 0.1 copy.42
  5.3 0.1 add_add_fusion
  5.3 0.1 add.46
  5.4 0.2 select_reduce_fusion.1
  5.6 0.1 copy.36
  5.7 0.1 select_reduce_fusion.2
  5.8 0.1 copy.37
  5.9 0.1 reshape.97.ids_ref
  6.0 0.6 select_reduce_fusion
  6.7 0.1 reshape.98
  6.8 1.5 copy.39
  8.3 0.7 copy.40
  8.9 0.0 copy-start.2
  9.0 1.5 copy-done.2
  10.5 0.0 copy-start.3
  10.5 1.5 copy-done.3
  12.0 0.0 copy-start.4
  12.0 1.4 copy-done.4
  13.4 191.2 %shard_map.73 = (bf16[65,512,128]{2,1,0:T(8,128)(2,1)S(1)}, bf16[4,8,4,2,2,128,128]{6,5,4,3,2,1,0:T(8,128)(2,1)}, bf16[4,8,6,128,128]{4,3,2,1,0:T(8,128)(2,1)S(1)}, s32[8,8,128]{2,1,0:T(8,128)S(1)}) custom-call(s32[32]{0:T(128)S(1)} %reshape.97.ids_ref, s32[8,8,128]{2,1,0:T(8,128)S(1)} %bitcast.12, bf16[8,512,128]{2,1,0:T(8,128)(2,1)S(1)} %bitcast.11, ...), custom_call_target="tpu_custom_call" | custom-call | tf_op jit(solution)/shard_map/pallas_call | solution.py:202
  204.6 0.0 copy-start
  204.6 3.3 %copy-done = bf16[65,512,128]{2,1,0:T(8,128)(2,1)} copy-done((bf16[65,512,128]{2,1,0:T(8,128)(2,1)}, bf16[65,512,128]{2,1,0:T(8,128)(2,1)S(1)}, u32[]{:S(2)}) %copy-start) | copy-done | bytes 8519704
  207.8 0.0 copy-start.1
  207.9 2.7 %copy-done.1 = bf16[4,8,6,128,128]{4,3,2,1,0:T(8,128)(2,1)} copy-done((bf16[4,8,6,128,128]{4,3,2,1,0:T(8,128)(2,1)}, bf16[4,8,6,128,128]{4,3,2,1,0:T(8,128)(2,1)S(1)}, u32[]{:S(2)}) %copy-start.1) | copy-done | bytes 6291480
  210.6 0.1 reshape.102.rows_ref
  210.6 33.1 %shard_map.74 = bf16[512,1024]{1,0:T(8,128)(2,1)} custom-call(s32[512]{0:T(512)S(1)} %reshape.102.rows_ref, s32[192]{0:T(256)S(1)} %compare_select_fusion.1.places_ref, bf16[65,512,128]{2,1,0:T(8,128)(2,1)} %copy-done, bf16[4,8,4,2,2,128,128]{6,5,4,3,2,1,0:T(8,128)(2,1)} %get-tuple-element.11.got_ref, bf16[4,8,6,128,128]{4,3,2,1,0:T(8,128)(2,1)} %copy-done.1), custom_call_target="tpu_custom_call" | custom-call | tf_op jit(solution)/shard_map/pallas_call | solution.py:262
  (11 shorter events, 0.1 us)
Async XLA Ops:
  8.9 1.5 copy-start.2
  10.5 1.5 copy-start.3
  12.0 1.4 copy-start.4
  204.6 3.3 %copy-start = (bf16[65,512,128]{2,1,0:T(8,128)(2,1)}, bf16[65,512,128]{2,1,0:T(8,128)(2,1)S(1)}, u32[]{:S(2)}) copy-start(bf16[65,512,128]{2,1,0:T(8,128)(2,1)S(1)} %get-tuple-element.10.feat_ref) | copy-start | bytes 25559044
  207.8 2.7 %copy-start.1 = (bf16[4,8,6,128,128]{4,3,2,1,0:T(8,128)(2,1)}, bf16[4,8,6,128,128]{4,3,2,1,0:T(8,128)(2,1)S(1)}, u32[]{:S(2)}) copy-start(bf16[4,8,6,128,128]{4,3,2,1,0:T(8,128)(2,1)S(1)} %get-tuple-element.12.down_ref) | copy-start | bytes 18874372

commit v2 on v1

v2 whole, which is shorter than its diff:
```python
import functools

import jax
import jax.numpy as jnp
from jax import lax
from jax.experimental import pallas as pl
from jax.experimental.pallas import tpu as pltpu
from jax.sharding import PartitionSpec as P

MESH = pl.DeviceIdType.MESH
FIRST = 2
EARLY = 3


def layer_kernel(
    sizes, ids_ref, spots_ref, rows_ref, tok_ref, gate_hbm, up_hbm, down_ref, out_ref,
    feat_ref, got_ref, down_out, rows_out, lists, hidden, gate_ref, up_ref,
    sel, zr_s, zr_r, zl_s, zl_r, y_s, y_r, wx_s, wx_r, li_s, li_r, xs_s, xs_r, sib_s, sib_r, loc,
):
    nt, nw, cap, kg, kd = sizes
    xs, ys = nt // 2, nt // 2
    zs = nw // ys
    t, w = lax.axis_index("tok"), lax.axis_index("wa")
    x, c = lax.div(t, 2), lax.rem(t, 2)
    z, y = lax.div(w, ys), lax.rem(w, ys)
    fb, row_count, blk = tok_ref.shape
    loads = [
        pltpu.make_async_copy(gate_hbm, gate_ref, loc.at[0]),
        pltpu.make_async_copy(up_hbm, up_ref, loc.at[1]),
    ]
    for copy in loads:
        copy.start()

    barrier = pltpu.get_barrier_semaphore()
    for r in range(1, nw):
        pl.semaphore_signal(barrier, inc=1, device_id=(t, lax.rem(w + r, nw)), device_id_type=MESH)
    for r in range(1, nt):
        pl.semaphore_signal(barrier, inc=1, device_id=(lax.rem(t + r, nt), w), device_id_type=MESH)
    pl.semaphore_wait(barrier, nw + nt - 2)

    def remote(src, dst, ssem, rsem, dev):
        return pltpu.make_async_remote_copy(
            src_ref=src, dst_ref=dst, send_sem=ssem, recv_sem=rsem, device_id=dev, device_id_type=MESH
        )

    def feat(src):
        return feat_ref.at[pl.ds(src * fb, fb)]

    def right(k, src):
        return remote(src, feat(w - (k - 1) * ys), zr_s.at[k - 1], zr_r.at[k - 1], (t, w + ys))

    def left(k, src):
        return remote(src, feat(w + (k - 1) * ys), zl_s.at[k - 1], zl_r.at[k - 1], (t, w - ys))

    def across(zz, dy, src):
        return remote(
            src, feat(zz * ys + y), y_s.at[zz, dy - 1], y_r.at[zz, dy - 1], (t, z * ys + lax.rem(y + dy, ys))
        )

    def send_right(k, src):
        pl.when((z + 1 < zs) & (z - (k - 1) >= 0))(lambda: right(k, src).start())

    def send_left(k, src):
        pl.when((z >= 1) & (z + (k - 1) < zs))(lambda: left(k, src).start())

    send_right(1, tok_ref)
    send_left(1, tok_ref)
    for dy in range(1, ys):
        across(z, dy, tok_ref).start()

    def sibling(j, e, src, dst):
        return remote(src, dst, sib_s.at[j, e], sib_r.at[j, e], (x * 2 + (1 - c), w))

    def along_x(j, dx, src, dst):
        return remote(src, dst, xs_s.at[j, dx - 1], xs_r.at[j, dx - 1], (lax.rem(x + dx, xs) * 2 + c, w))

    def source(j):
        return lax.rem(w + nw - j, nw)

    def slot(j, tt):
        return got_ref.at[tt, source(j)]

    def down_slot(j, tt):
        return down_out.at[tt]

    def from_x(dx, core):
        return lax.rem(x + xs - dx, xs) * 2 + core

    def spread(j, src, at=slot):
        for dx in range(1, xs):
            along_x(j, dx, src, at(j, t)).start()
        sibling(j, 0, src, at(j, t)).start()

    spread(nw, down_ref, down_slot)

    def pick(d):
        for s in range(cap):
            chosen = ids_ref[d * cap + s]
            sel[d, s, 0] = gate_ref[chosen]
            sel[d, s, 1] = up_ref[chosen]

    for copy in loads:
        copy.wait()
    pick(w)
    spread(0, sel.at[w])
    own_copies = [
        pltpu.make_async_copy(tok_ref, feat(w), loc.at[2]),
        pltpu.make_async_copy(down_ref, down_out.at[t], loc.at[3]),
        pltpu.make_async_copy(sel.at[w], got_ref.at[t, w], loc.at[4]),
        pltpu.make_async_copy(rows_ref.at[w], rows_out.at[w], loc.at[5]),
    ]
    for copy in own_copies:
        copy.start()

    def to_dest(r):
        d = lax.rem(w + r, nw)
        return remote(sel.at[d], got_ref.at[t, w], wx_s.at[r - 1], wx_r.at[r - 1], (t, d))

    def rows_to_dest(r):
        d = lax.rem(w + r, nw)
        return remote(rows_ref.at[d], rows_out.at[w], li_s.at[r - 1], li_r.at[r - 1], (t, d))

    @pl.loop(1, nw)
    def _(r):
        rows_to_dest(r).start()
        pick(lax.rem(w + r, nw))

    feat_ref[nw * fb] = jnp.zeros((row_count, blk), feat_ref.dtype)
    hidden[nw * cap] = jnp.zeros((row_count, blk), hidden.dtype)

    first = -(-(nw - 1) * FIRST // 8)
    per = -(-(nw - 1 - first) // (zs - 1))

    def batch(lo, hi):
        for r in range(lo, min(hi, nw)):
            to_dest(r).start()

    batch(1, 1 + first)

    def forward_tokens(k):
        @pl.when(z - k >= 0)
        def _():
            block = feat(w - k * ys)
            remote(block, block, zr_s.at[k - 1], zr_r.at[k - 1], (t, w)).wait_recv()
            if k < zs - 1:
                send_right(k + 1, block)
            for dy in range(1, ys):
                across(z - k, dy, block).start()

        @pl.when(z + k < zs)
        def _():
            block = feat(w + k * ys)
            remote(block, block, zl_s.at[k - 1], zl_r.at[k - 1], (t, w)).wait_recv()
            if k < zs - 1:
                send_left(k + 1, block)
            for dy in range(1, ys):
                across(z + k, dy, block).start()

    def forward_weights(j):
        to_me = slot(j, t)
        remote(to_me, to_me, wx_s.at[j - 1], wx_r.at[j - 1], (t, w)).wait_recv()
        spread(j, to_me)

    def forward_sibling(j, at=slot):
        for dx in range(1, xs):
            there = at(j, from_x(dx, c))
            along_x(j, dx, there, there).wait_recv()
            sibling(j, dx, there, there).start()

    def wait_sibling(j, at=slot):
        for e in range(xs):
            there = at(j, from_x(e, 1 - c))
            sibling(j, e, there, there).wait_recv()

    for k in range(1, zs):
        forward_tokens(k)
        batch(1 + first + (k - 1) * per, 1 + first + k * per)
    early = min(EARLY, nw - 1)
    for j in range(1, early + 1):
        forward_weights(j)
    forward_sibling(nw, down_slot)
    forward_sibling(0)
    for copy in own_copies:
        copy.wait()
    for zz in range(zs):
        for dy in range(1, ys):
            block = feat(zz * ys + lax.rem(y + ys - dy, ys))
            across(zz, dy, block).wait_recv()

    @pl.loop(1, nw)
    def _(r):
        row = rows_out.at[source(r)]
        remote(row, row, li_s.at[r - 1], li_r.at[r - 1], (t, w)).wait_recv()

    to_scalars = pltpu.make_async_copy(rows_out, lists, loc.at[6])
    to_scalars.start()
    to_scalars.wait()

    def column(origin, s, which):
        base = (s * 2 + which) * kg
        picks = [feat_ref[lists[origin, (base + k) // 128, (base + k) % 128]] for k in range(kg)]
        rhs = [got_ref[tt, origin, s, which].reshape(-1, blk) for tt in range(nt)]
        return jnp.dot(
            jnp.concatenate(picks, axis=1), jnp.concatenate(rhs, axis=0), preferred_element_type=jnp.float32
        )

    @pl.loop(0, nw)
    def _(i):
        pl.when(i + early + 1 < nw)(lambda: forward_weights(i + early + 1))
        pl.when(i + 1 < nw)(lambda: forward_sibling(i + 1))
        wait_sibling(i)
        origin = source(i)
        for s in range(cap):
            gate = column(origin, s, 0)
            up = column(origin, s, 1)
            hidden[origin * cap + s] = (gate / (1.0 + jnp.exp(-gate)) * up).astype(hidden.dtype)

    wait_sibling(nw, down_slot)
    for b in range(down_ref.shape[0]):
        lhs = jnp.concatenate([hidden[spots_ref[b * kd + k]] for k in range(kd)], axis=1)
        rhs = jnp.concatenate([down_out[tt, b].reshape(-1, blk) for tt in range(nt)], axis=0)
        out_ref[:, b * blk : (b + 1) * blk] = jnp.dot(lhs, rhs, preferred_element_type=jnp.float32).astype(
            out_ref.dtype
        )

    for k in range(1, zs):
        pl.when((z + 1 < zs) & (z - (k - 1) >= 0))(lambda: right(k, tok_ref).wait_send())
        pl.when((z >= 1) & (z + (k - 1) < zs))(lambda: left(k, tok_ref).wait_send())
    for zz in range(zs):
        for dy in range(1, ys):
            across(zz, dy, tok_ref).wait_send()

    @pl.loop(1, nw)
    def _(r):
        to_dest(r).wait_send()
        rows_to_dest(r).wait_send()

    def sent(j, at=slot):
        for dx in range(1, xs):
            along_x(j, dx, at(j, t), at(j, t)).wait_send()
        for e in range(xs):
            sibling(j, e, at(j, t), at(j, t)).wait_send()

    pl.loop(0, nw)(sent)
    sent(nw, down_slot)


def layer(sizes, ids, spots, rows, tokens, gate, up, down):
    nt, nw, cap, kg, kd = sizes
    fb, row_count, blk = tokens.shape
    slots, outs = gate.shape[1], down.shape[0]
    xs = ys = nt // 2
    zs = nw // ys
    sem = pltpu.SemaphoreType.DMA
    dtype = tokens.dtype
    any_spec = pl.BlockSpec(memory_space=pl.ANY)
    vmem_spec = pl.BlockSpec(memory_space=pltpu.VMEM)
    smem_spec = pl.BlockSpec(memory_space=pltpu.SMEM)
    return pl.pallas_call(
        functools.partial(layer_kernel, sizes),
        out_shape=jax.ShapeDtypeStruct((row_count, outs * blk), dtype),
        in_specs=[smem_spec, smem_spec, vmem_spec, any_spec, any_spec, any_spec, any_spec],
        out_specs=vmem_spec,
        scratch_shapes=[
            pltpu.VMEM((nw * fb + 1, row_count, blk), dtype),
            pltpu.VMEM((nt, nw, cap, 2, slots, blk, blk), dtype),
            pltpu.VMEM((nt, *down.shape), dtype),
            pltpu.VMEM(rows.shape, rows.dtype),
            pltpu.SMEM(rows.shape, rows.dtype),
            pltpu.VMEM((nw * cap + 1, row_count, blk), dtype),
            pltpu.VMEM(gate.shape, dtype),
            pltpu.VMEM(up.shape, dtype),
            pltpu.VMEM((nw, cap, 2, slots, blk, blk), dtype),
            sem((zs - 1,)), sem((zs - 1,)), sem((zs - 1,)), sem((zs - 1,)),
            sem((zs, ys - 1)), sem((zs, ys - 1)),
            sem((nw - 1,)), sem((nw - 1,)), sem((nw - 1,)), sem((nw - 1,)),
            sem((nw + 1, xs - 1)), sem((nw + 1, xs - 1)), sem((nw + 1, xs)), sem((nw + 1, xs)),
            sem((7,)),
        ],
        compiler_params=pltpu.CompilerParams(
            collective_id=0, has_side_effects=True, vmem_limit_bytes=60 << 20
        ),
    )(ids, spots, rows, tokens, gate, up, down)


def running(flags):
    upto = jnp.arange(flags.shape[1])
    upto = upto[:, None] >= upto[None, :]
    return jnp.sum((flags[:, None, :] & upto[None]).astype(jnp.int32), axis=2)


def on_device(tokens, gate_weight, up_weight, down_weight, gate_list, up_list, down_list):
    nt, nw = lax.axis_size("tok"), lax.axis_size("wa")
    me = lax.axis_index("wa")
    hid_blocks, _, blk, _ = gate_weight.shape
    outs = down_weight.shape[0]
    kd, kg = down_list.shape[1], gate_list.shape[1]
    cap = max(2, (kd + nw - 1) // nw + 1)
    row_count = tokens.shape[0]
    fb = tokens.shape[1] // blk
    groups = down_list.reshape(nw, -1)

    own_ids = me * hid_blocks + jnp.arange(hid_blocks, dtype=jnp.int32)
    wanted = jnp.any(groups[:, :, None] == own_ids[None, None, :], axis=1)
    places = running(wanted) - 1
    chosen = wanted[:, None, :] & (places[:, None, :] == jnp.arange(cap, dtype=jnp.int32)[None, :, None])
    ids = jnp.sum(jnp.where(chosen, jnp.arange(hid_blocks, dtype=jnp.int32), 0), axis=2)
    both = jnp.concatenate([gate_list, up_list], axis=1)
    both = jnp.where(both < 0, nw * fb, both)
    picked = jnp.sum(jnp.where(chosen[..., None], both[None, None], 0), axis=2).reshape(nw, -1)
    width = -(-picked.shape[1] // 1024) * 1024
    rows = jnp.pad(picked, ((0, 0), (0, width - picked.shape[1]))).reshape(nw, -1, 128)

    mine = lax.dynamic_slice_in_dim(down_list, me * outs, outs, 0)
    all_ids = jnp.arange(nw * hid_blocks, dtype=jnp.int32)
    hit = mine.reshape(-1)[:, None] == all_ids[None, :]
    named = jnp.any(hit, axis=0).reshape(nw, hid_blocks)
    spot = running(named) - 1 + cap * jnp.arange(nw, dtype=jnp.int32)[:, None]
    spots = jnp.sum(jnp.where(hit, spot.reshape(1, -1), 0), axis=1)
    spots = jnp.where(mine.reshape(-1) >= 0, spots, nw * cap)

    blocks = jnp.transpose(tokens.reshape(row_count, fb, blk), (1, 0, 2))
    return layer(
        (nt, nw, cap, kg, kd), ids.reshape(-1), spots, rows, blocks, gate_weight, up_weight, down_weight
    )


def solution(mesh):
    placed = (
        P("tok", "wa"),
        P("wa", "tok", None, None),
        P("wa", "tok", None, None),
        P("wa", "tok", None, None),
        P("wa", None),
        P("wa", None),
        P(),
    )
    return jax.shard_map(
        on_device, mesh=mesh, in_specs=placed, out_specs=P("tok", "wa"), check_vma=False
    )
```

time: 244 us -> 270 us (1.11)
  the two profiles are of different devices: /device:TPU:0 before, /device:TPU:28 now
where the time goes in v2:
time: 270 us
  Pallas kernels  256 us (95%)
  local copies, waits for them, and re-layouts  10.1 us (4%)
  other arithmetic  3.43 us (1%)
    pallas_call x1, Pallas kernels, layer(): pl.pallas_call(functools.partial(layer_kernel, sizes), out_shape=jax.Shap...  256 us
    unnamed x6, local copies, waits for them, and re-layouts  5.86 us

profile of v2, /device:TPU:28, one launch (start us, length us, event | category | flops | bytes accessed | tf_op | source)
XLA Modules:
  0.0 269.6 jit_solution(1368571017583407319)
XLA Ops:
  0.0 0.7 constant_dynamic-update-slice_fusion.1
  0.7 0.7 constant_dynamic-update-slice_fusion
  1.4 0.8 constant_dynamic-slice_fusion
  2.2 0.1 copy.38
  2.3 0.1 reshape.92
  2.3 0.1 fusion
  2.5 0.1 and.46
  2.5 0.8 copy.33
  3.3 0.1 eq.45
  3.4 0.6 compare_reduce_fusion
  4.1 0.1 copy.34
  4.2 1.0 convert_reduce_fusion
  5.2 0.1 copy.39
  5.3 0.1 add_add_fusion
  5.3 0.1 add.46
  5.4 0.2 select_reduce_fusion.1
  5.6 0.6 compare_select_fusion.1.spots_ref
  6.2 0.1 copy.36
  6.3 0.1 select_reduce_fusion.2
  6.4 0.1 copy.37
  6.5 0.7 reshape.91.ids_ref
  7.2 0.6 select_reduce_fusion
  7.8 0.1 reshape.93
  7.9 0.6 copy.45
  8.5 1.5 copy.41
  10.0 1.3 copy.42
  11.3 256.0 %shard_map.73 = bf16[512,1024]{1,0:T(8,128)(2,1)} custom-call(s32[32]{0:T(128)} %reshape.91.ids_ref, s32[192]{0:T(256)} %compare_select_fusion.1.spots_ref, s32[8,8,128]{2,1,0:T(8,128)} %bitcast.9, bf16[8,512,128]{2,1,0:T(8,128)(2,1)} %bitcast.8, bf16[28,2,128,128]{3,2,1,0:T(8,128)(2,1)} %gate_hbm.1, bf16[28,2,128,128]{3,2,1,0:T(8,128)(2,1)} %up_hbm.1, ...), custom_call_target="tpu_custom_call" | custom-call | tf_op jit(solution)/shard_map/pallas_call | solution.py:259
  267.3 2.3 copy.48
  (7 shorter events, 0.0 us)

commit v3 on v1

--- a/solution.py
+++ b/solution.py
@@ -11,9 +11,9 @@
 
 
 def exchange_kernel(
-    sizes, ids_ref, rows_ref, tok_ref, gate_ref, up_ref, down_ref,
+    sizes, ids_ref, rows_ref, tok_ref, gate_hbm, up_hbm, down_ref,
     feat_ref, got_ref, down_out, rows_out,
-    sel, zero, zr_s, zr_r, zl_s, zl_r, y_s, y_r, wx_s, wx_r, li_s, li_r, xs_s, xs_r, sib_s, sib_r, loc,
+    gate_ref, up_ref, sel, zero, zr_s, zr_r, zl_s, zl_r, y_s, y_r, wx_s, wx_r, li_s, li_r, xs_s, xs_r, sib_s, sib_r, loc,
 ):
     nt, nw, cap = sizes
     xs, ys = nt // 2, nt // 2
@@ -22,6 +22,12 @@
     x, c = lax.div(t, 2), lax.rem(t, 2)
     z, y = lax.div(w, ys), lax.rem(w, ys)
     fb = tok_ref.shape[0]
+    loads = [
+        pltpu.make_async_copy(gate_hbm, gate_ref, loc.at[5]),
+        pltpu.make_async_copy(up_hbm, up_ref, loc.at[6]),
+    ]
+    for copy in loads:
+        copy.start()
 
     barrier = pltpu.get_barrier_semaphore()
     for r in range(1, nw):
@@ -99,6 +105,8 @@
             sel[d, s, 0] = gate_ref[chosen]
             sel[d, s, 1] = up_ref[chosen]
 
+    for copy in loads:
+        copy.wait()
     pick(w)
     own_copies[3].start()
     own_copies[4].start()
@@ -198,7 +206,6 @@
     sem = pltpu.SemaphoreType.DMA
     dtype = tokens.dtype
     any_spec = pl.BlockSpec(memory_space=pl.ANY)
-    vmem_spec = pl.BlockSpec(memory_space=pltpu.VMEM)
     return pl.pallas_call(
         functools.partial(exchange_kernel, sizes),
         out_shape=(
@@ -207,27 +214,31 @@
             jax.ShapeDtypeStruct((nt, *down.shape), dtype),
             jax.ShapeDtypeStruct(rows.shape, rows.dtype),
         ),
-        in_specs=[pl.BlockSpec(memory_space=pltpu.SMEM), any_spec, any_spec, vmem_spec, vmem_spec, any_spec],
+        in_specs=[pl.BlockSpec(memory_space=pltpu.SMEM), any_spec, any_spec, any_spec, any_spec, any_spec],
         out_specs=(any_spec,) * 4,
         scratch_shapes=[
+            pltpu.VMEM(gate.shape, dtype),
+            pltpu.VMEM(up.shape, dtype),
             pltpu.VMEM((nw, cap, 2, slots, blk, blk), dtype),
             pltpu.VMEM((row_count, blk), dtype),
             sem((zs - 1,)), sem((zs - 1,)), sem((zs - 1,)), sem((zs - 1,)),
             sem((zs, ys - 1)), sem((zs, ys - 1)),
             sem((nw - 1,)), sem((nw - 1,)), sem((nw - 1,)), sem((nw - 1,)),
             sem((nw + 1, xs - 1)), sem((nw + 1, xs - 1)), sem((nw + 1, xs)), sem((nw + 1, xs)),
-            sem((5,)),
+            sem((7,)),
         ],
         compiler_params=pltpu.CompilerParams(
-            collective_id=0, has_side_effects=True, vmem_limit_bytes=24 << 20
+            collective_id=0, has_side_effects=True, vmem_limit_bytes=60 << 20
         ),
     )(ids, rows, tokens, gate, up, down)
 
 
-def layer_kernel(sizes, rows_ref, places_ref, feat_ref, got_ref, down_ref, out_ref, hidden):
+def layer_kernel(sizes, rows_ref, places_ref, feat_ref, got_ref, down_hbm, out_ref, hidden, down_ref, down_sem):
     nt, nw, cap, kg, kd, none = sizes
     step = pl.program_id(0)
     blk = feat_ref.shape[2]
+
+    load = pltpu.make_async_copy(down_hbm, down_ref, down_sem)
 
     def column(s, which):
         base = ((step * cap + s) * 2 + which) * kg
@@ -237,6 +248,7 @@
 
     @pl.when(step == 0)
     def _():
+        load.start()
         hidden[nw * cap] = jnp.zeros(hidden.shape[1:], hidden.dtype)
 
     for s in range(cap):
@@ -246,6 +258,7 @@
 
     @pl.when(step == nw - 1)
     def _():
+        load.wait()
         for b in range(out_ref.shape[1] // blk):
             lhs = jnp.concatenate([hidden[places_ref[b * kd + k]] for k in range(kd)], axis=1)
             rhs = jnp.concatenate([down_ref[tt, b].reshape(-1, blk) for tt in range(nt)], axis=0)
@@ -268,12 +281,16 @@
             in_specs=[
                 vmem_spec,
                 pl.BlockSpec((nt, 1, *got.shape[2:]), lambda i, a, b: (0, i, 0, 0, 0, 0, 0)),
-                vmem_spec,
+                pl.BlockSpec(memory_space=pl.ANY),
             ],
             out_specs=pl.BlockSpec((row_count, outs * blk), lambda i, a, b: (0, 0)),
-            scratch_shapes=[pltpu.VMEM((nw * cap + 1, row_count, blk), feat.dtype)],
+            scratch_shapes=[
+                pltpu.VMEM((nw * cap + 1, row_count, blk), feat.dtype),
+                pltpu.VMEM(down.shape, down.dtype),
+                pltpu.SemaphoreType.DMA,
+            ],
         ),
-        compiler_params=pltpu.CompilerParams(vmem_limit_bytes=48 << 20),
+        compiler_params=pltpu.CompilerParams(vmem_limit_bytes=58 << 20),
     )(rows, places, feat, got, down)
 
 

time: 244 us -> 237 us (0.971)
  local copies, waits for them, and re-layouts: 16.5 us -> 9.29 us
    unnamed x16 -> x6, local copies, waits for them, and re-layouts: 13.4 us -> 4.37 us
where the time goes in v3:
time: 237 us
  Pallas kernels  224 us (95%)
  local copies, waits for them, and re-layouts  9.29 us (4%)
  other arithmetic  3.46 us (1%)
    pallas_call x1, Pallas kernels, exchange(): pl.pallas_call(functools.partial(exchange_kernel, sizes), out_shape=(jax....  192 us
    pallas_call x1, Pallas kernels, layer(): pl.pallas_call(functools.partial(layer_kernel, sizes), out_shape=jax.Shap...  31.4 us

profile of v3, /device:TPU:0, one launch (start us, length us, event | category | flops | bytes accessed | tf_op | source)
XLA Modules:
  0.0 236.5 jit_solution(13203799879574864583)
XLA Ops:
  0.0 0.7 constant_dynamic-update-slice_fusion.1
  0.7 0.7 constant_dynamic-update-slice_fusion
  1.4 0.8 constant_dynamic-slice_fusion
  2.2 0.1 copy.41
  2.2 0.1 reshape.103
  2.3 0.1 fusion
  2.5 0.1 and.46
  2.5 0.8 copy.33
  3.3 0.1 eq.45
  3.4 0.6 compare_reduce_fusion
  4.0 0.1 copy.34
  4.1 1.0 convert_reduce_fusion
  5.2 0.1 copy.42
  5.3 0.1 add_add_fusion
  5.3 0.1 add.46
  5.4 0.2 select_reduce_fusion.1
  5.6 0.6 compare_select_fusion.1.places_ref
  6.2 0.1 copy.36
  6.3 0.1 select_reduce_fusion.2
  6.4 0.1 copy.37
  6.5 0.7 reshape.97.ids_ref
  7.2 0.6 select_reduce_fusion
  7.8 0.1 reshape.98
  7.9 0.6 copy.48
  8.5 1.5 copy.39
  10.0 1.3 copy.40
  11.4 192.3 %shard_map.73 = (bf16[65,512,128]{2,1,0:T(8,128)(2,1)}, bf16[4,8,4,2,2,128,128]{6,5,4,3,2,1,0:T(8,128)(2,1)}, bf16[4,8,6,128,128]{4,3,2,1,0:T(8,128)(2,1)}, s32[8,8,128]{2,1,0:T(8,128)}) custom-call(s32[32]{0:T(128)} %reshape.97.ids_ref, s32[8,8,128]{2,1,0:T(8,128)} %bitcast.13, bf16[8,512,128]{2,1,0:T(8,128)(2,1)} %bitcast.11, ...), custom_call_target="tpu_custom_call" | custom-call | tf_op jit(solution)/shard_map/pallas_call | solution.py:209
  203.7 0.8 copy.47
  204.4 0.7 reshape.102.rows_ref
  205.1 31.4 %shard_map.74 = bf16[512,1024]{1,0:T(8,128)(2,1)} custom-call(s32[512]{0:T(512)} %reshape.102.rows_ref, s32[192]{0:T(256)} %compare_select_fusion.1.places_ref, bf16[65,512,128]{2,1,0:T(8,128)(2,1)} %get-tuple-element.10.feat_ref, bf16[4,8,4,2,2,128,128]{6,5,4,3,2,1,0:T(8,128)(2,1)} %get-tuple-element.11.got_ref, ...), custom_call_target="tpu_custom_call" | custom-call | tf_op jit(solution)/shard_map/pallas_call | solution.py:275
  (8 shorter events, 0.0 us)
